TPU v7x, 256 devices: a whole 4x4x8 slice. The times are simulated.
256 devices in a mesh: section: 4 (over y_hi, core), expert: 64 (over x, y_lo, z).
Axes of the slice: x: 4, y: 4 (y_hi: 2, y_lo: 2; y = y_hi * 2 + y_lo), z: 8, core: 2. Of those that a mesh axis runs over, the one named last changes fastest.
Arguments:
- pending_groups: bfloat16 [4, 8192, 2048], P('section', 'expert'), may hold values from -6 to 6
- stratum_rescale_factors: float32 [4, 2048], P('section'), may hold values from 0.1 to 1.9
- ending_rescale_factor: float32 [2048], replicated, may hold values from 0.1 to 1.9
- assigned_specialists: int32 [4, 8192, 8], P('section', 'expert'), may hold values from 0 to 63, all different within a row; in each aligned block of 128 rows (0 to 127, 128 to 255, ..., all dimensions but the last counted through in order) at most 24 rows name the same one
- mixing_factors: float32 [4, 8192, 8], P('section', 'expert'), may hold values from 0.1 to 0.7
- specialist_raising_matrix: bfloat16 [4, 64, 2048, 1536], P('section', 'expert'), may hold values from -0.125 to 0.125
- specialist_lowering_matrix: bfloat16 [4, 64, 768, 2048], P('section', 'expert'), may hold values from -0.21875 to 0.21875
Outputs:
- arrived: bfloat16 [4, 8192, 2048], P('section', 'expert')
Inputs may be any that keep to these rules, and one draw needn't show every extreme that they name: `assigned_specialists`: within each aligned block of 128 tokens of one section (the tokens of one device), every expert is named by at most 24 tokens, a bound that some block reaches.
All inputs are finite; a program needn't handle non-finite values. Where the computation divides by a largest or mean magnitude, that divisor is 1e-20 or more.
Results may differ from a plain program's by a relative error of at most 0.0062.
Values may be sent and summed in bfloat16 or wider, within the bound.
A program may use at most 128 MiB of HBM per device.

v0:
```python
import jax
import jax.numpy as jnp
from jax import lax
from jax.sharding import PartitionSpec as P

BLOCK = 128


EPS = 1e-06


def from_behind(block, axis, distance):
    devices = range(lax.axis_size(axis))
    route = [((i - distance) % len(devices), i) for i in devices]
    return lax.ppermute(block, axis, route)


def rms_scale(values, norm_gain):
    widened = values.astype(jnp.float32)
    return (
        widened * lax.rsqrt(jnp.mean(widened * widened, axis=-1, keepdims=True) + EPS) * norm_gain
    )


def block_split(normed):
    lead_shape = normed.shape[:-1]
    blocks = normed.reshape(lead_shape + (-1, BLOCK))
    scales = (jnp.max(jnp.abs(blocks), axis=-1, keepdims=True) + EPS).astype(jnp.bfloat16)
    quantized = (blocks / scales.astype(jnp.float32)).astype(jnp.bfloat16)
    return (quantized, scales)


def restore_blocks(quantized, scales):
    restored = quantized.astype(jnp.float32) * scales.astype(jnp.float32)
    return restored.astype(jnp.bfloat16)


def local(
    pending_groups,
    stratum_rescale_factors,
    ending_rescale_factor,
    assigned_specialists,
    mixing_factors,
    specialist_raising_matrix,
    specialist_lowering_matrix,
):
    item_group = pending_groups[0]
    norm_gain = stratum_rescale_factors[0]
    routing = assigned_specialists[0]
    weight = mixing_factors[0]
    gate_up = specialist_raising_matrix[0]
    down = specialist_lowering_matrix[0]
    owners = lax.axis_size("expert")
    local_count = gate_up.shape[0]
    tok_count, top_count = routing.shape
    feature_width = item_group.shape[1]
    hidden_width = down.shape[1]
    experts_all = local_count * owners
    capacity = min(tok_count, max(2, 3 * tok_count * top_count // (2 * experts_all)))
    flat_route = routing.reshape(-1)
    onehot = (flat_route[:, None] == jnp.arange(experts_all, dtype=jnp.int32)[None, :]).astype(
        jnp.int32
    )
    before = jnp.cumsum(onehot, axis=0) - onehot
    slot_index = jnp.sum(before * onehot, axis=1)
    target = flat_route * capacity + slot_index

    def place_rows(rows):
        spread = jnp.repeat(rows, top_count, axis=0)
        empty = jnp.zeros((experts_all * capacity,) + rows.shape[1:], rows.dtype)
        return (
            empty.at[target].set(spread).reshape((owners, local_count, capacity) + rows.shape[1:])
        )

    quantized, scales = block_split(rms_scale(item_group, norm_gain))
    quant_rows = lax.all_to_all(
        place_rows(quantized.reshape(tok_count, feature_width)),
        "expert",
        split_axis=0,
        concat_axis=0,
        tiled=True,
    )
    scale_rows = lax.all_to_all(
        place_rows(scales[..., 0]), "expert", split_axis=0, concat_axis=0, tiled=True
    )
    lead_shape = quant_rows.shape[:-1]
    restored = restore_blocks(quant_rows.reshape(lead_shape + (-1, BLOCK)), scale_rows[..., None])
    experts_restored = restored.reshape(quant_rows.shape)
    gate_and_up = jnp.einsum(
        "sech,ehf->secf", experts_restored, gate_up, preferred_element_type=jnp.float32
    )
    hidden = (
        jax.nn.silu(gate_and_up[..., :hidden_width]) * gate_and_up[..., hidden_width:]
    ).astype(jnp.bfloat16)
    result = jnp.einsum("secf,efh->sech", hidden, down, preferred_element_type=jnp.float32).astype(
        jnp.bfloat16
    )
    returned_rows = lax.all_to_all(result, "expert", split_axis=0, concat_axis=0, tiled=True)
    picked = returned_rows.reshape(experts_all * capacity, feature_width)[target].reshape(
        tok_count, top_count, feature_width
    )
    mixture = jnp.sum(weight[..., None] * picked.astype(jnp.float32), axis=1)
    layer_out = (item_group.astype(jnp.float32) + mixture).astype(jnp.bfloat16)
    position = lax.axis_index("section")
    arriving = from_behind(layer_out, "section", 1)
    arrived = jnp.where(
        position == 0, rms_scale(arriving, ending_rescale_factor).astype(jnp.bfloat16), arriving
    )
    return arrived[None]


def solution(mesh):
    in_specs = (
        P("section", "expert", None),
        P("section", None),
        P(),
        P("section", "expert", None),
        P("section", "expert", None),
        P("section", "expert", None, None),
        P("section", "expert", None, None),
    )
    out_specs = P("section", "expert", None)
    return jax.shard_map(local, mesh=mesh, in_specs=in_specs, out_specs=out_specs, check_vma=False)
```

profile of v0, /device:TPU:1, one launch (start us, length us, event | category | flops | bytes accessed | tf_op | source)
XLA Modules:
  0.0 432.7 jit_solution(9508882618707540447)
XLA Ops:
  0.0 0.0 copy-start
  0.0 0.0 copy-start.1
  0.0 0.9 broadcast_multiply_fusion
  0.9 0.9 copy.35
  1.8 0.1 eq.33
  1.9 0.1 eq.29
  1.9 2.1 convert_bitcast_fusion.1
  4.1 1.2 fusion.24
  5.3 0.1 copy.34
  5.4 0.1 mul.113
  5.5 0.7 fusion.37
  6.2 31.1 %reduce-window.6 = s32[64,8,128]{2,1,0:T(8,128)S(1)} reduce-window(s32[64,8,128]{2,1,0:T(8,128)} %fusion.37, s32[]{:T(128)} %constant.13.clone.1), window={size=1x1x128 pad=0_0x0_0x127_0}, to_apply=%region_0.0 | reduce-window | flops 8323072 | bytes 524292 | tf_op jit(solution)/shard_map/reduce-window
  37.3 0.8 slice.18
  38.2 1.1 copy.37
  39.3 0.1 copy.38
  39.4 0.1 broadcast_add_fusion
  39.5 1.4 copy.46
  41.0 0.0 copy-done.1
  41.0 0.2 fusion.29
  41.2 0.3 abs_reduce_fusion
  41.5 0.6 add_convert_fusion
  42.1 0.1 fusion.34
  42.2 3.5 scatter_custom_fusion.1
  45.7 0.9 copy.40
  46.6 1.8 reshape.198
  48.4 13.5 %all-to-all-start.1 = ((bf16[64,2,192]{2,1,0:T(2,128)(2,1)}), bf16[64,2,192]{2,1,0:T(2,128)(2,1)S(1)}, u32[]{:S(2)}, u32[]{:S(2)}) async-start(bf16[64,2,192]{2,1,0:T(2,128)(2,1)} %reshape.198), calls=%async_computation.1 | async-start | bytes 131072 | tf_op jit(solution)/shard_map/all_to_all | solution.py:83
  61.9 1.1 div.22
  63.0 2.3 fusion.27
  65.3 10.7 %scatter_custom_fusion = bf16[1536,2048]{1,0:T(8,128)(2,1)} fusion(s32[1024]{0:T(1024)S(1)} %bitcast.117, bf16[]{:T(256)} %constant.8.clone.1, bf16[128,2048]{1,0:T(8,128)(2,1)} %fusion.27), kind=kCustom, calls=%fused_computation.13 | custom fusion | bytes 6815746 | tf_op jit(solution)/shard_map/scatter | solution.py:72
  76.0 0.0 all-to-all-done.1
  76.1 11.1 %all-to-all-start = ((bf16[64,1,24,2048]{3,2,1,0:T(8,128)(2,1)}), bf16[64,1,24,2048]{3,2,1,0:T(8,128)(2,1)}, u32[]{:S(2)}, u32[]{:S(2)}) async-start(bf16[64,1,24,2048]{3,2,1,0:T(8,128)(2,1)} %bitcast.107), calls=%async_computation | async-start | bytes 12582912 | tf_op jit(solution)/shard_map/all_to_all | solution.py:76
  87.2 0.2 reshape.199
  87.4 0.8 bitcast_convert_fusion
  88.2 2.2 copy.41
  90.4 8.4 %mul.126 = f32[64,24,16,128]{3,2,1,0:T(8,128)} broadcast(f32[64,24,16]{2,1,0:T(8,128)} %copy.41), dimensions={0,1,2} | broadcast | bytes 12681216 | tf_op jit(solution)/shard_map/mul | solution.py:34
  98.9 13.6 %mul.127 = f32[64,1,24,2048]{3,2,1,0:T(8,128)} reshape(f32[64,24,16,128]{3,2,1,0:T(8,128)} %mul.126) | data formatting | bytes 25165824 | tf_op jit(solution)/shard_map/mul | solution.py:34
  112.5 111.2 %all-to-all-done = bf16[64,1,24,2048]{3,2,1,0:T(8,128)(2,1)} async-done(((bf16[64,1,24,2048]{3,2,1,0:T(8,128)(2,1)}), bf16[64,1,24,2048]{3,2,1,0:T(8,128)(2,1)}, u32[]{:S(2)}, u32[]{:S(2)}) %all-to-all-start) | async-done | bytes 6291488 | tf_op jit(solution)/shard_map/all_to_all | solution.py:76
  223.7 14.9 %fusion.5 = f32[64,1,24,1536]{3,2,0,1:T(8,128)S(1)} fusion(bf16[1,1,2048,1536]{3,2,1,0:T(8,128)(2,1)} %param.12, f32[64,1,24,2048]{3,2,1,0:T(8,128)} %mul.127, bf16[64,1,24,2048]{3,2,1,0:T(8,128)(2,1)} %all-to-all-done), kind=kOutput, calls=%fused_computation.10 | convolution fusion | flops 9673113600 | bytes 34603008 | tf_op jit(solution)/shard_map/sech,ehf->secf/dot_general | solution.py:89
  238.6 0.0 copy-done
  238.6 7.4 %convert_bitcast_fusion = bf16[64,1,24,2048]{3,2,1,0:T(8,128)(2,1)} fusion(bf16[1,1,768,2048]{3,2,1,0:T(8,128)(2,1)S(1)} %copy-done, f32[64,1,24,1536]{3,2,0,1:T(8,128)S(1)} %fusion.5), kind=kOutput, calls=%fused_computation.9 | convolution fusion | flops 4842061824 | bytes 18874368 | tf_op jit(solution)/shard_map/secf,efh->sech/dot_general | solution.py:95
  246.0 0.0 copy-start.3
  246.0 11.4 %all-to-all-start.2 = ((bf16[64,1,24,2048]{3,2,1,0:T(8,128)(2,1)}), bf16[64,1,24,2048]{3,2,1,0:T(8,128)(2,1)}, u32[]{:S(2)}, u32[]{:S(2)}) async-start(bf16[64,1,24,2048]{3,2,1,0:T(8,128)(2,1)} %convert_bitcast_fusion), calls=%async_computation.2 | async-start | bytes 12582912 | tf_op jit(solution)/shard_map/all_to_all | solution.py:98
  257.4 0.0 copy-done.3
  257.4 0.1 copy.33
  257.5 136.6 %all-to-all-done.2 = bf16[64,1,24,2048]{3,2,1,0:T(8,128)(2,1)} async-done(((bf16[64,1,24,2048]{3,2,1,0:T(8,128)(2,1)}), bf16[64,1,24,2048]{3,2,1,0:T(8,128)(2,1)}, u32[]{:S(2)}, u32[]{:S(2)}) %all-to-all-start.2) | async-done | bytes 6291488 | tf_op jit(solution)/shard_map/all_to_all | solution.py:98
  394.1 12.4 %gather_fusion = bf16[1024,2048]{1,0:T(8,128)(2,1)} fusion(bf16[1536,2048]{1,0:T(8,128)(2,1)} %bitcast.28, s32[1024]{0:T(1024)S(1)} %broadcast_clamp_fusion), kind=kCustom, calls=%fused_computation | custom fusion | bytes 8392704 | tf_op jit(solution)/shard_map/gather | solution.py:99
  406.5 0.0 copy-start.2
  406.5 6.5 %fusion = f32[128,2048]{1,0:T(8,128)S(1)} fusion(bf16[1024,2048]{1,0:T(8,128)(2,1)} %gather_fusion, f32[128,8]{1,0:T(8,128)S(1)} %copy.33), kind=kLoop, calls=%fused_computation.5 | loop fusion | flops 6029312 | bytes 5246976 | tf_op jit(solution)/shard_map/reduce_sum | solution.py:102
  413.0 2.0 fusion.28
  415.0 7.8 %collective-permute-start = (bf16[128,2048]{1,0:T(8,128)(2,1)}, bf16[128,2048]{1,0:T(8,128)(2,1)}, u32[]{:S(2)}, u32[]{:S(2)}) collective-permute-start(bf16[128,2048]{1,0:T(8,128)(2,1)} %fusion.28), channel_id=1, source_target_pairs={{192,0},{0,64},{64,128},{128,192},{193,1},{1,65},{65,129},{129,193... | collective-permute-start | bytes 1572872 | tf_op jit(solution)/shard_map/ppermute | solution.py:15
  422.7 6.4 %collective-permute-done = bf16[128,2048]{1,0:T(8,128)(2,1)} collective-permute-done((bf16[128,2048]{1,0:T(8,128)(2,1)}, bf16[128,2048]{1,0:T(8,128)(2,1)}, u32[]{:S(2)}, u32[]{:S(2)}) %collective-permute-start) | collective-permute-done | bytes 524320 | tf_op jit(solution)/shard_map/ppermute | solution.py:15
  429.2 1.2 fusion.21
  430.4 0.0 copy-done.2
  430.4 2.3 fusion.31
  (6 shorter events, 0.1 us)
Async XLA Ops:
  0.0 238.6 %copy-start = (bf16[1,1,768,2048]{3,2,1,0:T(8,128)(2,1)S(1)}, bf16[1,1,768,2048]{3,2,1,0:T(8,128)(2,1)}, u32[]{:S(2)}) copy-start(bf16[1,1,768,2048]{3,2,1,0:T(8,128)(2,1)} %param.13) | copy-start | bytes 9437188
  0.0 41.0 %copy-start.1 = (f32[1,2048]{1,0:T(1,128)S(1)}, f32[1,2048]{1,0:T(1,128)}, u32[]{:S(2)}) copy-start(f32[1,2048]{1,0:T(1,128)} %param.8) | copy-start | bytes 24580
  48.4 27.6 %all-to-all-start.1 = ((bf16[64,2,192]{2,1,0:T(2,128)(2,1)}), bf16[64,2,192]{2,1,0:T(2,128)(2,1)S(1)}, u32[]{:S(2)}, u32[]{:S(2)}) async-start(bf16[64,2,192]{2,1,0:T(2,128)(2,1)} %reshape.198), calls=%async_computation.1 | async-start | bytes 131072 | tf_op jit(solution)/shard_map/all_to_all | solution.py:83
  76.1 147.6 %all-to-all-start = ((bf16[64,1,24,2048]{3,2,1,0:T(8,128)(2,1)}), bf16[64,1,24,2048]{3,2,1,0:T(8,128)(2,1)}, u32[]{:S(2)}, u32[]{:S(2)}) async-start(bf16[64,1,24,2048]{3,2,1,0:T(8,128)(2,1)} %bitcast.107), calls=%async_computation | async-start | bytes 12582912 | tf_op jit(solution)/shard_map/all_to_all | solution.py:76
  246.0 11.4 %copy-start.3 = (f32[1,128,8]{1,2,0:T(8,128)S(1)}, f32[1,128,8]{1,2,0:T(8,128)}, u32[]{:S(2)}) copy-start(f32[1,128,8]{1,2,0:T(8,128)} %param.11) | copy-start | bytes 12292
  246.0 148.1 %all-to-all-start.2 = ((bf16[64,1,24,2048]{3,2,1,0:T(8,128)(2,1)}), bf16[64,1,24,2048]{3,2,1,0:T(8,128)(2,1)}, u32[]{:S(2)}, u32[]{:S(2)}) async-start(bf16[64,1,24,2048]{3,2,1,0:T(8,128)(2,1)} %convert_bitcast_fusion), calls=%async_computation.2 | async-start | bytes 12582912 | tf_op jit(solution)/shard_map/all_to_all | solution.py:98
  406.5 23.9 %copy-start.2 = (f32[2048]{0:T(1024)S(1)}, f32[2048]{0:T(1024)}, u32[]{:S(2)}) copy-start(f32[2048]{0:T(1024)} %param.9) | copy-start | bytes 24580
  415.0 14.2 %collective-permute-start = (bf16[128,2048]{1,0:T(8,128)(2,1)}, bf16[128,2048]{1,0:T(8,128)(2,1)}, u32[]{:S(2)}, u32[]{:S(2)}) collective-permute-start(bf16[128,2048]{1,0:T(8,128)(2,1)} %fusion.28), channel_id=1, source_target_pairs={{192,0},{0,64},{64,128},{128,192},{193,1},{1,65},{65,129},{129,193... | collective-permute-start | bytes 1572872 | tf_op jit(solution)/shard_map/ppermute | solution.py:15
where the time goes:
time: 435 us; the launch traced here: 433 us
  waiting for transfers between devices  254 us (58%)
  local copies, waits for them, and re-layouts  59.7 us (14%)
  other arithmetic  52.6 us (12%)
  starting transfers between devices  43.8 us (10%)
  matrix products  22.3 us (5%)
    all_to_all x1, waiting for transfers between devices, local(): lax.all_to_all(result, 'expert', split_axis=0, concat_axis=0, tiled=True)  137 us
    all_to_all x1, waiting for transfers between devices, local(): lax.all_to_all(place_rows(quantized.reshape(tok_count, feature_width)), '...  111 us
    another operation x3, other arithmetic  31.3 us
    mul x2, local copies, waits for them, and re-layouts, restore_blocks(): restored = quantized.astype(jnp.float32) * scales.astype(jnp.float32)  22 us
    dot_general x1, matrix products, local(): jnp.einsum('sech,ehf->secf', experts_restored, gate_up, preferred_element...  14.9 us
    scatter x2, local copies, waits for them, and re-layouts, place_rows(): empty.at[target].set(spread)  14.2 us
    all_to_all x1, starting transfers between devices, local(): lax.all_to_all(place_rows(scales[..., 0]), 'expert', split_axis=0, concat...  13.5 us
    gather x1, local copies, waits for them, and re-layouts, local(): returned_rows.reshape(experts_all * capacity, feature_width)[target]  12.4 us
  transfers between devices with their start and end apart: 4, of which 3 were waited for; matrix products, arithmetic and copies ran while one was open for 9% of the time, Pallas kernels for 0%

commit v1 on v0

v1 whole, which is shorter than its diff:
```python
import jax
import jax.numpy as jnp
from jax import lax
from jax.sharding import PartitionSpec as P

BLOCK = 128
EPS = 1e-06
NZ = 8
CAPACITY = 24


def rms_scale(values, norm_gain):
    widened = values.astype(jnp.float32)
    return (
        widened * lax.rsqrt(jnp.mean(widened * widened, axis=-1, keepdims=True) + EPS) * norm_gain
    )


def restore_rows(normed):
    blocks = normed.reshape(normed.shape[0], -1, BLOCK)
    scales = (jnp.max(jnp.abs(blocks), axis=-1, keepdims=True) + EPS).astype(jnp.bfloat16)
    scales = scales.astype(jnp.float32)
    quantized = (blocks / scales).astype(jnp.bfloat16)
    restored = quantized.astype(jnp.float32) * scales
    return restored.astype(jnp.bfloat16).reshape(normed.shape)


def local(pending, gain, final_gain, assigned, mixing, raising, lowering):
    item_group = pending[0]
    routing = assigned[0]
    weight = mixing[0]
    gate_up = raising[0, 0]
    down = lowering[0, 0]
    owners = lax.axis_size("expert")
    planes = NZ
    columns = owners // planes
    tok_count, top = routing.shape
    width = item_group.shape[1]
    hidden_width = down.shape[0]
    line_groups = [[c * planes + z for z in range(planes)] for c in range(columns)]
    plane_groups = [[c * planes + z for c in range(columns)] for z in range(planes)]
    plane = lax.axis_index("expert") % planes

    chosen = routing[:, :, None] == jnp.arange(owners, dtype=jnp.int32)
    named = jnp.any(chosen, axis=1)
    share = jnp.sum(jnp.where(chosen, weight[:, :, None], 0.0), axis=1)
    earlier = jnp.tril(jnp.ones((tok_count, tok_count), jnp.bfloat16), -1)
    slot = jnp.dot(earlier, named.astype(jnp.bfloat16), preferred_element_type=jnp.float32)
    slot = jnp.where(named, slot, -1.0)
    restored = restore_rows(rms_scale(item_group, gain[0]))
    packet = jnp.concatenate(
        [restored, slot.astype(jnp.bfloat16), share.astype(jnp.bfloat16)], axis=1
    )
    line = lax.all_gather(packet, "expert", axis_index_groups=line_groups)

    def of_plane(part):
        return lax.dynamic_index_in_dim(
            part.reshape(planes, tok_count, columns, planes), plane, 3, keepdims=False
        )

    slots = of_plane(line[:, :, width : width + owners])
    shares = of_plane(line[:, :, width + owners :])
    match = slots[..., None] == jnp.arange(CAPACITY, dtype=jnp.bfloat16)
    pick = match.astype(jnp.bfloat16)
    mix = jnp.where(match, shares[..., None], 0)
    rows = jnp.einsum(
        "btjc,bth->jbch", pick, line[:, :, :width], preferred_element_type=jnp.float32
    ).astype(jnp.bfloat16)
    rows = lax.all_to_all(
        rows, "expert", split_axis=0, concat_axis=0, tiled=True, axis_index_groups=plane_groups
    ).reshape(-1, width)
    both = jnp.dot(rows, gate_up, preferred_element_type=jnp.float32)
    hidden = (jax.nn.silu(both[:, :hidden_width]) * both[:, hidden_width:]).astype(jnp.bfloat16)
    result = jnp.dot(hidden, down, preferred_element_type=jnp.float32).astype(jnp.bfloat16)
    result = lax.all_to_all(
        result.reshape(columns, planes, CAPACITY, width),
        "expert",
        split_axis=0,
        concat_axis=0,
        tiled=True,
        axis_index_groups=plane_groups,
    )
    partial = jnp.einsum(
        "btjc,jbch->bth", mix, result, preferred_element_type=jnp.float32
    ).astype(jnp.bfloat16)
    partial = partial.reshape(planes * tok_count, width)
    mixture = lax.psum_scatter(
        partial, "expert", scatter_dimension=0, axis_index_groups=line_groups, tiled=True
    )
    layer_out = (item_group.astype(jnp.float32) + mixture.astype(jnp.float32)).astype(jnp.bfloat16)
    sections = lax.axis_size("section")
    arriving = lax.ppermute(
        layer_out, "section", [(i, (i + 1) % sections) for i in range(sections)]
    )
    arrived = jnp.where(
        lax.axis_index("section") == 0,
        rms_scale(arriving, final_gain).astype(jnp.bfloat16),
        arriving,
    )
    return arrived[None]


def solution(mesh):
    in_specs = (
        P("section", "expert", None),
        P("section", None),
        P(),
        P("section", "expert", None),
        P("section", "expert", None),
        P("section", "expert", None, None),
        P("section", "expert", None, None),
    )
    out_specs = P("section", "expert", None)
    return jax.shard_map(local, mesh=mesh, in_specs=in_specs, out_specs=out_specs, check_vma=False)
```

time: 435 us -> 372 us (0.86)
  blocking collectives: 0 us -> 76.2 us
  local copies, waits for them, and re-layouts: 59.7 us -> 10.7 us
  waiting for transfers between devices: 254 us -> 208 us
  starting transfers between devices: 43.8 us -> 8.02 us
  other arithmetic: 52.6 us -> 22.6 us
  between operations: 0.15 us -> 13.6 us
  matrix products: 22.3 us -> 32 us
    all_to_all x3 -> x1, waiting for transfers between devices: 248 us -> 86.2 us  [local(): lax.all_to_all(result.reshape(columns, planes, CAPACITY, width), 'expert'...]
    all_to_all x0 -> x1, blocking collectives: none -> 76.2 us  [local(): lax.all_to_all(rows, 'expert', split_axis=0, concat_axis=0, tiled=True, a...]
    all_gather x0 -> x1, waiting for transfers between devices: none -> 61.2 us  [local(): line = lax.all_gather(packet, 'expert', axis_index_groups=line_groups)]
    reduce_scatter x0 -> x1, waiting for transfers between devices: none -> 53.9 us  [local(): lax.psum_scatter(partial, 'expert', scatter_dimension=0, axis_index_group...]
    another operation x3 -> x0, other arithmetic: 31.3 us -> none
    all_to_all x3 -> x1, starting transfers between devices: 36 us -> 4.74 us  [local(): lax.all_to_all(result.reshape(columns, planes, CAPACITY, width), 'expert'...]
    mul x5 -> x0, local copies, waits for them, and re-layouts: 22.3 us -> none  [the longest x2 22 us: restore_blocks(): restored = quantized.astype(jnp.float32) * scales.astype(jnp.float32)]
    scatter x2 -> x0, local copies, waits for them, and re-layouts: 14.2 us -> none  [place_rows(): empty.at[target].set(spread)]
  transfers between devices with their start and end apart: 4 -> 4, of which waited for: 3 -> 4; matrix products, arithmetic and copies ran while one was open for 9% -> 0% of each run, Pallas kernels for 0% -> 0%
where the time goes in v1:
time: 372 us; the launch traced here: 371 us
  waiting for transfers between devices  208 us (56%)
  blocking collectives  76.2 us (20%)
  matrix products  32 us (9%)
  other arithmetic  22.6 us (6%)
  between operations  13.6 us (4%)
  local copies, waits for them, and re-layouts  10.7 us (3%)
  starting transfers between devices  8.02 us (2%)
    all_to_all x1, waiting for transfers between devices, local(): lax.all_to_all(result.reshape(columns, planes, CAPACITY, width), 'expert'...  86.2 us
    all_to_all x1, blocking collectives, local(): lax.all_to_all(rows, 'expert', split_axis=0, concat_axis=0, tiled=True, a...  76.2 us
    all_gather x1, waiting for transfers between devices, local(): line = lax.all_gather(packet, 'expert', axis_index_groups=line_groups)  61.2 us
    reduce_scatter x1, waiting for transfers between devices, local(): lax.psum_scatter(partial, 'expert', scatter_dimension=0, axis_index_group...  53.9 us
    dot_general x1, matrix products, local(): both = jnp.dot(rows, gate_up, preferred_element_type=jnp.float32)  10.1 us
    unnamed x1, matrix products  8.54 us
    convert_element_type x1, other arithmetic, local(): rows = jnp.einsum('btjc,bth->jbch', pick, line[:, :, :width], preferred_e...  8.18 us
  transfers between devices with their start and end apart: 4, of which 4 were waited for; matrix products, arithmetic and copies ran while one was open for 0% of the time, Pallas kernels for 0%

profile of v1, /device:TPU:1, one launch (start us, length us, event | category | flops | bytes accessed | tf_op | source)
XLA Modules:
  0.0 370.9 jit_solution(14207009544768533518)
XLA Ops:
  6.5 0.0 copy-start
  6.5 0.0 copy-start.1
  6.5 0.0 all-gather.3.cloned.1.call-start
  6.5 1.4 fusion.19
  7.9 2.1 convert_bitcast_fusion.1
  10.1 0.7 fusion.29
  10.8 0.2 fusion.15
  11.0 0.1 copy.41
  11.1 0.7 select_reduce_fusion
  11.9 0.1 copy.42
  12.0 1.4 copy.50
  13.4 1.0 fusion.25
  14.5 0.3 abs_reduce_fusion
  14.8 0.1 copy.39
  14.9 0.1 copy.40
  15.0 0.3 div.22
  15.3 0.0 copy-done.1
  15.3 2.4 fusion.24
  17.7 1.8 concatenate.3
  19.5 0.0 all-gather.3.cloned.1.call-update
  19.6 61.2 %all-gather.3.cloned.1.call-done = bf16[1024,2176]{1,0:T(8,128)(2,1)} async-done(((bf16[128,2176]{1,0:T(8,128)(2,1)}), bf16[1024,2176]{1,0:T(8,128)(2,1)}) %all-gather.3.cloned.1.call-update) | async-done | bytes 4456464 | tf_op jit(solution)/shard_map/all_gather | solution.py:54
  80.8 1.9 fusion.43
  82.6 1.1 copy.43
  83.8 0.1 iota_compare_fusion
  83.9 8.5 %fusion.5 = f32[8,2048,192]{1,2,0} fusion(pred[8,128,192]{1,2,0:T(8,128)(4,1)S(1)} %bitcast.76, bf16[8,128,2176]{2,1,0:T(8,128)(2,1)} %bitcast.74), kind=kOutput, calls=%fused_computation.9 | convolution fusion | flops 805306368 | bytes 16973824
  92.5 8.2 %convert_bitcast_fusion = bf16[8,8,24,2048]{3,2,0,1:T(8,128)(2,1)} fusion(f32[8,2048,8,24]{1,3,2,0:T(8,128)} %bitcast.69), kind=kLoop, calls=%fused_computation.6 | loop fusion | flops 3145728 | bytes 18874368 | tf_op jit(solution)/shard_map/convert_element_type | solution.py:68
  100.6 0.0 slice-start
  100.6 3.5 copy.45
  104.2 0.0 slice-start.1
  104.2 76.2 %all_to_all.10 = bf16[8,8,24,2048]{3,2,1,0:T(8,128)(2,1)S(1)} all-to-all(bf16[8,8,24,2048]{3,2,1,0:T(8,128)(2,1)S(1)} %copy.45), channel_id=1, replica_groups={{0,8,16,24,32,40,48,56},{1,9,17,25,33,41,49,57},{2,10,18,26,34,42,50,58..., dimensions={0} | all-to-all | bytes 12582912 | tf_op jit(solution)/shard_map/all_to_all | solution.py:69
  180.3 0.0 slice-done
  180.3 0.0 slice-done.1
  180.3 10.1 %fusion = f32[1536,1536]{1,0:T(8,128)S(1)} fusion(bf16[1536,2048]{1,0:T(8,128)(2,1)S(1)} %bitcast.72, bf16[1,1,2048,1536]{3,2,1,0:T(8,128)(2,1)S(1)} %bitcast.88), kind=kOutput, calls=%fused_computation.2 | convolution fusion | flops 9663676416 | bytes 22020096 | tf_op jit(solution)/shard_map/dot_general | solution.py:72
  190.5 0.0 copy-done
  190.5 7.0 %convolution_convert_fusion = bf16[1536,2048]{1,0:T(8,128)(2,1)} fusion(bf16[1,1,768,2048]{3,2,1,0:T(8,128)(2,1)S(1)} %copy-done, f32[1536,1536]{1,0:T(8,128)S(1)} %fusion), kind=kOutput, calls=%fused_computation.1 | convolution fusion | flops 4842061824 | bytes 18874368 | tf_op jit(solution)/shard_map/dot_general | solution.py:74
  197.5 4.7 %all-to-all-start.1 = ((bf16[8,8,24,2048]{3,2,1,0:T(8,128)(2,1)}), bf16[8,8,24,2048]{3,2,1,0:T(8,128)(2,1)}, u32[]{:S(2)}, u32[]{:S(2)}) async-start(bf16[8,8,24,2048]{3,2,1,0:T(8,128)(2,1)} %bitcast.71), calls=%async_computation.1 | async-start | bytes 12582912 | tf_op jit(solution)/shard_map/all_to_all | solution.py:75
  202.2 0.0 reduce-scatter.2.cloned.1.call-start
  202.3 0.1 copy.44
  202.5 86.2 %all-to-all-done.1 = bf16[8,8,24,2048]{3,2,1,0:T(8,128)(2,1)} async-done(((bf16[8,8,24,2048]{3,2,1,0:T(8,128)(2,1)}), bf16[8,8,24,2048]{3,2,1,0:T(8,128)(2,1)}, u32[]{:S(2)}, u32[]{:S(2)}) %all-to-all-start.1) | async-done | bytes 6291488 | tf_op jit(solution)/shard_map/all_to_all | solution.py:75
  288.7 6.1 %bitcast_convert_fusion = bf16[8,128,2048]{2,1,0:T(8,128)(2,1)} fusion(bf16[8,8,24,2048]{3,2,1,0:T(8,128)(2,1)} %all-to-all-done.1, bf16[8,128,8]{1,2,0:T(8,128)(2,1)S(1)} %bitcast.81, bf16[8,128,8]{1,2,0:T(8,128)(2,1)S(1)} %bitcast.78), kind=kOutput, calls=%fused_computation | convolution fusion | flops 808189952 | bytes 10518528 | tf_op jit(solution)/shard_map/btjc,jbch->bth/dot_general | solution.py:83
  294.9 0.0 copy-start.2
  294.9 0.0 reduce-scatter.2.cloned.1.call-update
  294.9 53.9 %reduce-scatter.2.cloned.1.call-done = bf16[128,2048]{1,0:T(8,128)(2,1)} async-done(((bf16[1024,2048]{1,0:T(8,128)(2,1)}), bf16[128,2048]{1,0:T(8,128)(2,1)}) %reduce-scatter.2.cloned.1.call-update) | async-done | bytes 524304 | tf_op jit(solution)/shard_map/reduce_scatter | solution.py:87
  348.8 2.1 fusion.23
  350.9 3.2 collective-permute-start
  354.2 6.4 %collective-permute-done = bf16[128,2048]{1,0:T(8,128)(2,1)} collective-permute-done((bf16[128,2048]{1,0:T(8,128)(2,1)}, bf16[128,2048]{1,0:T(8,128)(2,1)}, u32[]{:S(2)}, u32[]{:S(2)}) %collective-permute-start) | collective-permute-done | bytes 524320 | tf_op jit(solution)/shard_map/ppermute | solution.py:92
  360.6 1.2 fusion.16
  361.8 0.0 copy-done.2
  361.8 2.3 fusion.27
  (9 shorter events, 0.1 us)
Async XLA Ops:
  6.5 184.0 %copy-start = (bf16[1,1,768,2048]{3,2,1,0:T(8,128)(2,1)S(1)}, bf16[1,1,768,2048]{3,2,1,0:T(8,128)(2,1)}, u32[]{:S(2)}) copy-start(bf16[1,1,768,2048]{3,2,1,0:T(8,128)(2,1)} %param.13) | copy-start | bytes 9437188
  6.5 8.8 %copy-start.1 = (f32[1,2048]{1,0:T(1,128)S(1)}, f32[1,2048]{1,0:T(1,128)}, u32[]{:S(2)}) copy-start(f32[1,2048]{1,0:T(1,128)} %param.8) | copy-start | bytes 24580
  6.5 74.2 %all-gather.3.cloned.1.call-start = ((), (), s32[]{:S(2)}) async-start(), calls=%async_computation.4 | async-start | bytes 5013504 | tf_op jit(solution)/shard_map/all_gather | solution.py:54
  100.6 79.7 %slice-start = ((s8[6291456]{0:T(1024)(128)(4,1)}), s8[4194304]{0:T(1024)(128)(4,1)S(1)}, s32[]{:S(2)}) async-start(s8[6291456]{0:T(1024)(128)(4,1)} %bitcast.87), calls=%async_computation.5 | async-start | bytes 8388608
  104.2 76.2 %slice-start.1 = ((s8[6291456]{0:T(1024)(128)(4,1)}), s8[2097152]{0:T(1024)(128)(4,1)S(1)}, s32[]{:S(2)}) async-start(s8[6291456]{0:T(1024)(128)(4,1)} %bitcast.87), calls=%async_computation.6 | async-start | bytes 4194304
  197.5 91.2 %all-to-all-start.1 = ((bf16[8,8,24,2048]{3,2,1,0:T(8,128)(2,1)}), bf16[8,8,24,2048]{3,2,1,0:T(8,128)(2,1)}, u32[]{:S(2)}, u32[]{:S(2)}) async-start(bf16[8,8,24,2048]{3,2,1,0:T(8,128)(2,1)} %bitcast.71), calls=%async_computation.1 | async-start | bytes 12582912 | tf_op jit(solution)/shard_map/all_to_all | solution.py:75
  202.2 146.6 %reduce-scatter.2.cloned.1.call-start = ((), (), s32[]{:S(2)}) async-start(), calls=%async_computation.3 | async-start | bytes 4718592 | tf_op jit(solution)/shard_map/reduce_scatter | solution.py:87
  294.9 67.0 %copy-start.2 = (f32[2048]{0:T(1024)S(1)}, f32[2048]{0:T(1024)}, u32[]{:S(2)}) copy-start(f32[2048]{0:T(1024)} %param.9) | copy-start | bytes 24580
  350.9 9.7 %collective-permute-start = (bf16[128,2048]{1,0:T(8,128)(2,1)}, bf16[128,2048]{1,0:T(8,128)(2,1)}, u32[]{:S(2)}, u32[]{:S(2)}) collective-permute-start(bf16[128,2048]{1,0:T(8,128)(2,1)} %fusion.23), channel_id=1, source_target_pairs={{0,64},{64,128},{128,192},{192,0},{1,65},{65,129},{129,193},{193,1... | collective-permute-start | bytes 1572872 | tf_op jit(solution)/shard_map/ppermute | solution.py:92
Sparse Core Ops, SparseCore 0:
  19.7 61.0 all-gather.2
  295.0 53.7 reduce-scatter.1

commit v2 on v1

v2 whole, which is shorter than its diff:
```python
import functools

import jax
import jax.numpy as jnp
from jax import lax
from jax.experimental import pallas as pl
from jax.experimental.pallas import tpu as pltpu
from jax.sharding import PartitionSpec as P

MESH = pl.DeviceIdType.MESH
F32, BF16 = jnp.float32, jnp.bfloat16
BLOCK = 128
EPS = 1e-06
NX, NY, NZ = 4, 2, 8
PLANE = NX * NY
FAR = NZ // 2
CAPACITY = 24
PAIR = 2 * CAPACITY
ROWS = PLANE * PAIR
PARTS = 2
TILE = 256
LANES = 128


def dot(a, b):
    return jnp.dot(a, b, preferred_element_type=F32)


def dot_nt(a, b):
    return lax.dot_general(a, b, (((1,), (1,)), ((), ())), preferred_element_type=F32)


def body(
    x_ref, gain_ref, final_ref, route_ref, mixing_ref, up_ref, down_ref, out_ref,
    line, meta, srow, rrow, orow, ret, mix, pick, spread, spread_t, wup, wdown, hid,
    acc, rsout, rsin, layer, arrive,
    ag_send, ag_recv, am_send, am_recv, d_send, d_recv, r_send, r_recv,
    rs_send, rs_recv, sec_send, sec_recv, w_sem,
):
    tokens, width = x_ref.shape
    part = width // PARTS
    hidden = wdown.shape[0]
    top = route_ref.shape[1]
    per_part = part // BLOCK
    tiles = part // TILE
    experts = PLANE * NZ
    half = tokens // 2
    me = lax.axis_index("expert")
    section = lax.axis_index("section")
    sections = lax.axis_size("section")
    mx, my, mz = me // (NY * NZ), (me // NZ) % NY, me % NZ

    def in_plane(sign, offset):
        dx, dy = offset // NY, offset % NY
        return (((mx + sign * dx + NX) % NX) * NY + (my + dy) % NY) * NZ + mz

    column = me - mz
    around = (column + (mz + 1) % NZ, column + (mz + NZ - 1) % NZ)
    following = (section + 1) % sections
    previous = (section + sections - 1) % sections

    weights = [
        pltpu.make_async_copy(up_ref, wup, w_sem.at[0]),
        pltpu.make_async_copy(down_ref, wdown, w_sem.at[1]),
    ]
    for copy in weights:
        copy.start()

    barrier = pltpu.get_barrier_semaphore()

    def greet(offset, carry):
        pl.semaphore_signal(
            barrier, 1, device_id={"expert": in_plane(1, offset)}, device_id_type=MESH
        )
        return carry

    lax.fori_loop(1, PLANE, greet, 0)
    for peer in around:
        pl.semaphore_signal(barrier, 1, device_id={"expert": peer}, device_id_type=MESH)
    for peer in (following, previous):
        pl.semaphore_signal(barrier, 1, device_id={"section": peer}, device_id_type=MESH)

    squares = jnp.zeros((tokens, BLOCK), F32)
    for b in range(width // BLOCK):
        values = x_ref[:, b * BLOCK : (b + 1) * BLOCK].astype(F32)
        squares = squares + values * values
    inverse = lax.rsqrt(jnp.sum(squares, axis=1, keepdims=True) / width + EPS)

    def restore(b, carry):
        cols = pl.ds(pl.multiple_of(b * BLOCK, BLOCK), BLOCK)
        normed = x_ref[:, cols].astype(F32) * inverse * gain_ref[:, cols]
        scale = jnp.max(jnp.abs(normed), axis=1, keepdims=True) + EPS
        scale = scale.astype(BF16).astype(F32)
        quantized = (normed / scale).astype(BF16).astype(F32)
        place = pl.ds(pl.multiple_of((b % per_part) * BLOCK, BLOCK), BLOCK)
        line[b // per_part, 0, :, place] = (quantized * scale).astype(BF16)
        return carry

    lax.fori_loop(0, width // BLOCK, restore, 0)

    lane = lax.broadcasted_iota(jnp.int32, (tokens, LANES), 1)
    named = jnp.zeros((tokens, LANES), F32)
    share = jnp.zeros((tokens, LANES), F32)
    for k in range(top):
        name = route_ref[:, k : k + 1]
        named = named + jnp.where(lane == name, 1.0, 0.0)
        share = share + jnp.where(lane - experts == name, mixing_ref[:, k : k + 1], 0.0)
    up_to = lax.broadcasted_iota(jnp.int32, (tokens, tokens), 0)
    up_to = up_to >= lax.broadcasted_iota(jnp.int32, (tokens, tokens), 1)
    place = dot(jnp.where(up_to, 1.0, 0.0).astype(BF16), named.astype(BF16))
    meta[0] = jnp.where(lane < experts, place * named, share).astype(BF16)

    def slots(shape, dim):
        q = lax.broadcasted_iota(jnp.int32, shape, dim)
        offset = jnp.zeros(shape, jnp.int32)
        for i in range(1, PLANE):
            offset = offset + jnp.where(q >= i * PAIR, 1, 0)
        q = q - offset * PAIR
        second = jnp.where(q >= CAPACITY, 1, 0)
        return offset, second, q - second * CAPACITY

    def owner(offset):
        dx, dy = offset // NY if isinstance(offset, int) else offset >> 1, offset & 1
        return ((((mx + dx) & (NX - 1)) * NY) + ((my + dy) & (NY - 1))) * NZ + mz

    offset, second, _ = slots((LANES, ROWS), 1)
    expert = owner(offset)
    lane_of = lax.broadcasted_iota(jnp.int32, (LANES, ROWS), 0)
    for i in range(2):
        for j in range(2):
            hit = (lane_of == expert + j * experts) & (second == i)
            spread[2 * j + i] = jnp.where(hit, 1.0, 0.0).astype(BF16)
    offset, second, _ = slots((ROWS, LANES), 0)
    expert = owner(offset)
    lane_of = lax.broadcasted_iota(jnp.int32, (ROWS, LANES), 1)
    for i in range(2):
        hit = (lane_of == expert) & (second == i)
        spread_t[i] = jnp.where(hit, 1.0, 0.0).astype(BF16)

    def few(step, direction):
        if step < FAR - 1:
            return pl.ds(0, tokens)
        return pl.ds(direction * half, half)

    def gather(direction, step, h):
        source, target = ((NZ - step) % NZ, NZ - 1 - step) if direction == 0 else (step, step + 1)
        rows = few(step, direction)
        return pltpu.make_async_remote_copy(
            line.at[h, source, rows], line.at[h, target, rows],
            ag_send.at[direction, step, h], ag_recv.at[direction, step, h],
            device_id={"expert": around[direction]}, device_id_type=MESH,
        )

    def gather_meta(direction, step):
        source, target = ((NZ - step) % NZ, NZ - 1 - step) if direction == 0 else (step, step + 1)
        rows = few(step, direction)
        return pltpu.make_async_remote_copy(
            meta.at[source, rows], meta.at[target, rows],
            am_send.at[direction, step], am_recv.at[direction, step],
            device_id={"expert": around[direction]}, device_id_type=MESH,
        )

    def build(c, first, last):
        _, _, want = slots((ROWS, tokens), 0)
        want = (want + 1).astype(F32)
        for i, rel in enumerate((first, last)):
            found = dot_nt(spread_t[i], meta[rel])
            pick[:, i * tokens : (i + 1) * tokens] = jnp.where(found == want, 1.0, 0.0).astype(BF16)
        _, _, want = slots((tokens, ROWS), 1)
        want = (want + 1).astype(F32)
        for i, rel in enumerate((first, last)):
            found = dot(meta[rel], spread[i])
            weight = dot(meta[rel], spread[2 + i])
            mix[c, i * tokens : (i + 1) * tokens] = jnp.where(found == want, weight, 0.0).astype(BF16)

    def select(c, first, last, h):
        def tile(n, carry):
            cols = pl.ds(pl.multiple_of(n * TILE, TILE), TILE)
            both = jnp.concatenate([line[h, first, :, cols], line[h, last, :, cols]], axis=0)
            rows = dot(pick[...], both).astype(BF16)
            srow[h, c, :, cols] = rows
            rrow[h, c, pl.ds(0, PAIR), cols] = rows[:PAIR]
            return carry

        lax.fori_loop(0, tiles, tile, 0)

    def plane_copy(source, target, send, recv, sign, offset, c, h):
        rows = pl.ds(pl.multiple_of(offset * PAIR, 16), PAIR)
        return pltpu.make_async_remote_copy(
            source.at[h, c, rows], target.at[h, c, rows], send.at[c, h], recv.at[c, h],
            device_id={"expert": in_plane(sign, offset)}, device_id_type=MESH,
        )

    def plane_all(source, target, send, recv, c, h):
        rows = pl.ds(PAIR, ROWS - PAIR)
        return pltpu.make_async_remote_copy(
            source.at[h, c, rows], target.at[h, c, rows], send.at[c, h], recv.at[c, h],
            device_id={"expert": in_plane(1, 1)}, device_id_type=MESH,
        )

    def dispatch(c, h):
        def send(offset, carry):
            plane_copy(srow, rrow, d_send, d_recv, 1, offset, c, h).start()
            return carry

        lax.fori_loop(1, PLANE, send, 0)

    def give_back(c, h):
        def send(offset, carry):
            plane_copy(orow, ret, r_send, r_recv, -1, offset, c, h).start()
            return carry

        lax.fori_loop(1, PLANE, send, 0)

    dispatched = functools.partial(plane_all, srow, rrow, d_send, d_recv)
    given_back = functools.partial(plane_all, orow, ret, r_send, r_recv)

    def expert_rows(c):
        for h in range(PARTS):
            dispatched(c, h).wait_recv()

        def gate(n, carry):
            total = []
            for base in (0, hidden):
                cols = pl.ds(pl.multiple_of(base + n * TILE, TILE), TILE)
                total.append(
                    dot(rrow[0, c], wup[pl.ds(0, part), cols])
                    + dot(rrow[1, c], wup[pl.ds(part, part), cols])
                )
            g, u = total
            cols = pl.ds(pl.multiple_of(n * TILE, TILE), TILE)
            hid[:, cols] = (g / (1.0 + jnp.exp(-g)) * u).astype(BF16)
            return carry

        lax.fori_loop(0, hidden // TILE, gate, 0)

        def lower(n, carry):
            wide = pl.ds(pl.multiple_of(n * TILE, TILE), TILE)
            cols = pl.ds(pl.multiple_of((n % tiles) * TILE, TILE), TILE)
            rows = dot(hid[...], wdown[:, wide]).astype(BF16)
            orow[n // tiles, c, :, cols] = rows
            ret[n // tiles, c, pl.ds(0, PAIR), cols] = rows[:PAIR]
            return carry

        lax.fori_loop(0, PARTS * tiles, lower, 0)

    def scatter(direction, step, h):
        source = FAR - step if direction == 0 else FAR + step
        rows = pl.ds(0, tokens) if step else pl.ds(direction * half, half)
        return pltpu.make_async_remote_copy(
            rsout.at[h, source, rows], rsin.at[h, direction, step, rows],
            rs_send.at[direction, step, h], rs_recv.at[direction, step, h],
            device_id={"expert": around[direction]}, device_id_type=MESH,
        )

    def combine(c, h):
        step = FAR - c if c else 0
        given_back(c, h).wait_recv()
        if step:
            for direction in range(2):
                scatter(direction, step - 1, h).wait_recv()

        def tile(n, carry):
            cols = pl.ds(pl.multiple_of(n * TILE, TILE), TILE)
            wide = pl.ds(pl.multiple_of(h * part + n * TILE, TILE), TILE)
            sums = dot(mix[c], ret[h, c, :, cols])
            near, away = sums[:tokens], sums[tokens:]
            if step == 0:
                acc[h, :, cols] = near + x_ref[:, wide].astype(F32)
                rsout[h, FAR, :, cols] = away.astype(BF16)
                return carry
            if step == 1:
                low, high = pl.ds(0, half), pl.ds(half, half)
                rsout[h, c, low, cols] = (near[:half] + rsin[h, 0, 0, low, cols].astype(F32)).astype(BF16)
                rsout[h, c, high, cols] = near[half:].astype(BF16)
                rsout[h, NZ - c, low, cols] = away[:half].astype(BF16)
                rsout[h, NZ - c, high, cols] = (away[half:] + rsin[h, 1, 0, high, cols].astype(F32)).astype(BF16)
                return carry
            rsout[h, c, :, cols] = (near + rsin[h, 0, step - 1, :, cols].astype(F32)).astype(BF16)
            rsout[h, NZ - c, :, cols] = (away + rsin[h, 1, step - 1, :, cols].astype(F32)).astype(BF16)
            return carry

        lax.fori_loop(0, tiles, tile, 0)
        for direction in range(2):
            scatter(direction, step, h).start()

    def onward(h):
        return pltpu.make_async_remote_copy(
            layer.at[h], arrive.at[h], sec_send.at[h], sec_recv.at[h],
            device_id={"section": following}, device_id_type=MESH,
        )

    pl.semaphore_wait(barrier, PLANE - 1 + 4)

    for direction in range(2):
        gather_meta(direction, 0).start()
    for h in range(PARTS):
        for direction in range(2):
            gather(direction, 0, h).start()
    for step in range(1, FAR + 1):
        c = step % FAR
        first, last = (step, NZ - step) if c else (0, FAR)
        for direction in range(2):
            gather_meta(direction, step - 1).wait_recv()
            if c:
                gather_meta(direction, step).start()
        build(c, first, last)
        for h in range(PARTS):
            for direction in range(2):
                gather(direction, step - 1, h).wait_recv()
                if c:
                    gather(direction, step, h).start()
            select(c, first, last, h)
            dispatch(c, h)

    for copy in weights:
        copy.wait()
    for c in range(1, FAR):
        expert_rows(c)
    for h in range(PARTS):
        give_back(FAR - 1, h)
    expert_rows(0)
    for h in range(PARTS):
        give_back(0, h)
    for c in range(FAR - 2, 0, -1):
        for h in range(PARTS):
            give_back(c, h)
    for c in (0, *range(FAR - 1, 0, -1)):
        for h in range(PARTS):
            combine(c, h)
    for h in range(PARTS):
        for direction in range(2):
            scatter(direction, FAR - 1, h).wait_recv()
        total = acc[h] + rsin[h, 0, FAR - 1].astype(F32) + rsin[h, 1, FAR - 1].astype(F32)
        layer[h] = total.astype(BF16)
        onward(h).start()
    for h in range(PARTS):
        onward(h).wait_recv()

    @pl.when(section != 0)
    def _():
        for h in range(PARTS):
            out_ref[:, h * part : (h + 1) * part] = arrive[h]

    @pl.when(section == 0)
    def _():
        squares = jnp.zeros((tokens, BLOCK), F32)
        for b in range(width // BLOCK):
            place = (b % per_part) * BLOCK
            values = arrive[b // per_part, :, place : place + BLOCK].astype(F32)
            squares = squares + values * values
        inverse = lax.rsqrt(jnp.sum(squares, axis=1, keepdims=True) / width + EPS)
        for b in range(width // BLOCK):
            place, cols = (b % per_part) * BLOCK, slice(b * BLOCK, (b + 1) * BLOCK)
            values = arrive[b // per_part, :, place : place + BLOCK].astype(F32)
            out_ref[:, cols] = (values * inverse * final_ref[:, cols]).astype(BF16)

    for h in range(PARTS):
        for step in range(FAR):
            for direction in range(2):
                gather(direction, step, h).wait_send()
                scatter(direction, step, h).wait_send()
        for c in range(FAR):
            dispatched(c, h).wait_send()
            given_back(c, h).wait_send()
        onward(h).wait_send()
    for step in range(FAR):
        for direction in range(2):
            gather_meta(direction, step).wait_send()


def local(pending, gain, final_gain, assigned, mixing, raising, lowering):
    x = pending[0]
    tokens, width = x.shape
    hidden = lowering.shape[2]
    part = width // PARTS
    vmem = pl.BlockSpec(memory_space=pltpu.VMEM)
    hbm = pl.BlockSpec(memory_space=pl.ANY)
    sems = pltpu.SemaphoreType.DMA
    arrived = pl.pallas_call(
        body,
        out_shape=jax.ShapeDtypeStruct((tokens, width), BF16),
        in_specs=[vmem, vmem, vmem, vmem, vmem, hbm, hbm],
        out_specs=vmem,
        scratch_shapes=[
            pltpu.VMEM((PARTS, NZ, tokens, part), BF16),
            pltpu.VMEM((NZ, tokens, LANES), BF16),
            pltpu.VMEM((PARTS, FAR, ROWS, part), BF16),
            pltpu.VMEM((PARTS, FAR, ROWS, part), BF16),
            pltpu.VMEM((PARTS, FAR, ROWS, part), BF16),
            pltpu.VMEM((PARTS, FAR, ROWS, part), BF16),
            pltpu.VMEM((FAR, 2 * tokens, ROWS), BF16),
            pltpu.VMEM((ROWS, 2 * tokens), BF16),
            pltpu.VMEM((4, LANES, ROWS), BF16),
            pltpu.VMEM((2, ROWS, LANES), BF16),
            pltpu.VMEM((width, 2 * hidden), BF16),
            pltpu.VMEM((hidden, width), BF16),
            pltpu.VMEM((ROWS, hidden), BF16),
            pltpu.VMEM((PARTS, tokens, part), F32),
            pltpu.VMEM((PARTS, NZ, tokens, part), BF16),
            pltpu.VMEM((PARTS, 2, FAR, tokens, part), BF16),
            pltpu.VMEM((PARTS, tokens, part), BF16),
            pltpu.VMEM((PARTS, tokens, part), BF16),
            sems((2, FAR, PARTS)),
            sems((2, FAR, PARTS)),
            sems((2, FAR)),
            sems((2, FAR)),
            sems((FAR, PARTS)),
            sems((FAR, PARTS)),
            sems((FAR, PARTS)),
            sems((FAR, PARTS)),
            sems((2, FAR, PARTS)),
            sems((2, FAR, PARTS)),
            sems((PARTS,)),
            sems((PARTS,)),
            sems((2,)),
        ],
        compiler_params=pltpu.CompilerParams(
            collective_id=0, has_side_effects=True, vmem_limit_bytes=62 << 20
        ),
        name="relay_step",
    )(x, gain, final_gain[None], assigned[0], mixing[0], raising[0, 0], lowering[0, 0])
    return arrived[None]


def solution(mesh):
    in_specs = (
        P("section", "expert", None),
        P("section", None),
        P(),
        P("section", "expert", None),
        P("section", "expert", None),
        P("section", "expert", None, None),
        P("section", "expert", None, None),
    )
    out_specs = P("section", "expert", None)
    return jax.shard_map(local, mesh=mesh, in_specs=in_specs, out_specs=out_specs, check_vma=False)
```

time: 372 us -> 177 us (0.48)
  waiting for transfers between devices: 208 us -> 0 us
  Pallas kernels: 0 us -> 169 us
  blocking collectives: 76.2 us -> 0 us
  matrix products: 32 us -> 0 us
  other arithmetic: 22.6 us -> 0 us
  between operations: 13.6 us -> 0.01 us
  starting transfers between devices: 8.02 us -> 0 us
  local copies, waits for them, and re-layouts: 10.7 us -> 4.7 us
    pallas_call x0 -> x1, Pallas kernels: none -> 169 us  [local(): pl.pallas_call(body, out_shape=jax.ShapeDtypeStruct((tokens, width), BF16...]
    all_to_all x1 -> x0, waiting for transfers between devices: 86.2 us -> none  [local(): lax.all_to_all(result.reshape(columns, planes, CAPACITY, width), 'expert'...]
    all_to_all x1 -> x0, blocking collectives: 76.2 us -> none  [local(): lax.all_to_all(rows, 'expert', split_axis=0, concat_axis=0, tiled=True, a...]
    all_gather x1 -> x0, waiting for transfers between devices: 61.2 us -> none  [local(): line = lax.all_gather(packet, 'expert', axis_index_groups=line_groups)]
    reduce_scatter x1 -> x0, waiting for transfers between devices: 53.9 us -> none  [local(): lax.psum_scatter(partial, 'expert', scatter_dimension=0, axis_index_group...]
    dot_general x4 -> x0, matrix products: 23.4 us -> none  [the longest x1 10.1 us: local(): both = jnp.dot(rows, gate_up, preferred_element_type=jnp.float32)]
    convert_element_type x4 -> x0, other arithmetic: 12.7 us -> none  [the longest x1 8.18 us: local(): rows = jnp.einsum('btjc,bth->jbch', pick, line[:, :, :width], preferred_e...]
    unnamed x1 -> x0, matrix products: 8.54 us -> none
  transfers between devices with their start and end apart: 4 -> 0, of which waited for: 4 -> 0; matrix products, arithmetic and copies ran while one was open for 0% -> 0% of each run, Pallas kernels for 0% -> 0%
where the time goes in v2:
time: 177 us; the launch traced here: 174 us
  Pallas kernels  169 us (95%)
  local copies, waits for them, and re-layouts  4.7 us (3%)
    pallas_call x1, Pallas kernels, local(): pl.pallas_call(body, out_shape=jax.ShapeDtypeStruct((tokens, width), BF16...  169 us
    unnamed x3, local copies, waits for them, and re-layouts  4.7 us

profile of v2, /device:TPU:1, one launch (start us, length us, event | category | flops | bytes accessed | tf_op | source)
XLA Modules:
  0.0 173.7 jit_solution(6015258329504445815)
XLA Ops:
  0.0 1.4 copy.8
  1.4 1.4 copy.9
  2.8 168.9 %relay_step.1 = bf16[128,2048]{1,0:T(8,128)(2,1)} custom-call(bf16[128,2048]{1,0:T(8,128)(2,1)} %bitcast.10, f32[1,2048]{1,0:T(1,128)} %gain_ref.1, f32[1,2048]{1,0:T(1,128)} %bitcast.13, s32[128,8]{1,0:T(8,128)} %bitcast.11, f32[128,8]{1,0:T(8,128)} %bitcast.12, bf16[2048,1536]{1,0:T(8,128)(2,1)} %bitcast.7, bf16[768,2048]{1,0:T(8,128)(2,1)} %bitcast.8), custom_call_target="tpu_custom_call" | custom-call | tf_op jit(solution)/shard_map/relay_step/pallas_call | solution.py:380
  171.8 1.9 %copy.11 = bf16[1,128,2048]{2,1,0:T(8,128)(2,1)} copy(bf16[1,128,2048]{2,1,0:T(8,128)(2,1)} %bitcast.9) | data formatting | bytes 1048576

commit v3 on v2

--- a/solution.py
+++ b/solution.py
@@ -17,8 +17,9 @@
 CAPACITY = 24
 PAIR = 2 * CAPACITY
 ROWS = PLANE * PAIR
-PARTS = 2
+PARTS = 4
 TILE = 256
+EARLY = 16
 LANES = 128
 
 
@@ -32,7 +33,7 @@
 
 def body(
     x_ref, gain_ref, final_ref, route_ref, mixing_ref, up_ref, down_ref, out_ref,
-    line, meta, srow, rrow, orow, ret, mix, pick, spread, spread_t, wup, wdown, hid,
+    line, meta, srow, rrow, orow, ret, erow, mix, pick, spread, spread_t, wup, wdown, hid,
     acc, rsout, rsin, layer, arrive,
     ag_send, ag_recv, am_send, am_recv, d_send, d_recv, r_send, r_recv,
     rs_send, rs_recv, sec_send, sec_recv, w_sem,
@@ -40,7 +41,7 @@
     tokens, width = x_ref.shape
     part = width // PARTS
     hidden = wdown.shape[0]
-    top = route_ref.shape[1]
+    top = route_ref.shape[0]
     per_part = part // BLOCK
     tiles = part // TILE
     experts = PLANE * NZ
@@ -80,35 +81,28 @@
     for peer in (following, previous):
         pl.semaphore_signal(barrier, 1, device_id={"section": peer}, device_id_type=MESH)
 
-    squares = jnp.zeros((tokens, BLOCK), F32)
-    for b in range(width // BLOCK):
-        values = x_ref[:, b * BLOCK : (b + 1) * BLOCK].astype(F32)
-        squares = squares + values * values
-    inverse = lax.rsqrt(jnp.sum(squares, axis=1, keepdims=True) / width + EPS)
-
-    def restore(b, carry):
-        cols = pl.ds(pl.multiple_of(b * BLOCK, BLOCK), BLOCK)
-        normed = x_ref[:, cols].astype(F32) * inverse * gain_ref[:, cols]
-        scale = jnp.max(jnp.abs(normed), axis=1, keepdims=True) + EPS
-        scale = scale.astype(BF16).astype(F32)
-        quantized = (normed / scale).astype(BF16).astype(F32)
-        place = pl.ds(pl.multiple_of((b % per_part) * BLOCK, BLOCK), BLOCK)
-        line[b // per_part, 0, :, place] = (quantized * scale).astype(BF16)
-        return carry
-
-    lax.fori_loop(0, width // BLOCK, restore, 0)
-
-    lane = lax.broadcasted_iota(jnp.int32, (tokens, LANES), 1)
-    named = jnp.zeros((tokens, LANES), F32)
-    share = jnp.zeros((tokens, LANES), F32)
-    for k in range(top):
-        name = route_ref[:, k : k + 1]
-        named = named + jnp.where(lane == name, 1.0, 0.0)
-        share = share + jnp.where(lane - experts == name, mixing_ref[:, k : k + 1], 0.0)
-    up_to = lax.broadcasted_iota(jnp.int32, (tokens, tokens), 0)
-    up_to = up_to >= lax.broadcasted_iota(jnp.int32, (tokens, tokens), 1)
-    place = dot(jnp.where(up_to, 1.0, 0.0).astype(BF16), named.astype(BF16))
-    meta[0] = jnp.where(lane < experts, place * named, share).astype(BF16)
+    def restore(h):
+        for b in range(h * per_part, (h + 1) * per_part):
+            cols = slice(b * BLOCK, (b + 1) * BLOCK)
+            normed = x_ref[:, cols].astype(F32) * inverse * gain_ref[:, cols]
+            scale = jnp.max(jnp.abs(normed), axis=1, keepdims=True) + EPS
+            scale = scale.astype(BF16).astype(F32)
+            quantized = (normed * (1.0 / scale)).astype(BF16).astype(F32)
+            place = slice((b % per_part) * BLOCK, (b % per_part + 1) * BLOCK)
+            line[h, 0, :, place] = (quantized * scale).astype(BF16)
+
+    def route():
+        lane = lax.broadcasted_iota(jnp.int32, (LANES, tokens), 0)
+        named = jnp.zeros((LANES, tokens), F32)
+        share = jnp.zeros((LANES, tokens), F32)
+        for k in range(top):
+            name = route_ref[k : k + 1, :]
+            named = named + jnp.where(lane == name, 1.0, 0.0)
+            share = share + jnp.where(lane - experts == name, mixing_ref[k : k + 1, :], 0.0)
+        up_to = lax.broadcasted_iota(jnp.int32, (tokens, tokens), 0)
+        up_to = up_to <= lax.broadcasted_iota(jnp.int32, (tokens, tokens), 1)
+        place = dot(named.astype(BF16), jnp.where(up_to, 1.0, 0.0).astype(BF16))
+        meta[0] = jnp.where(lane < experts, place * named, share).T.astype(BF16)
 
     def slots(shape, dim):
         q = lax.broadcasted_iota(jnp.int32, shape, dim)
@@ -120,22 +114,30 @@
         return offset, second, q - second * CAPACITY
 
     def owner(offset):
-        dx, dy = offset // NY if isinstance(offset, int) else offset >> 1, offset & 1
+        dx, dy = offset >> 1, offset & 1
         return ((((mx + dx) & (NX - 1)) * NY) + ((my + dy) & (NY - 1))) * NZ + mz
 
-    offset, second, _ = slots((LANES, ROWS), 1)
-    expert = owner(offset)
-    lane_of = lax.broadcasted_iota(jnp.int32, (LANES, ROWS), 0)
-    for i in range(2):
-        for j in range(2):
-            hit = (lane_of == expert + j * experts) & (second == i)
-            spread[2 * j + i] = jnp.where(hit, 1.0, 0.0).astype(BF16)
-    offset, second, _ = slots((ROWS, LANES), 0)
-    expert = owner(offset)
-    lane_of = lax.broadcasted_iota(jnp.int32, (ROWS, LANES), 1)
-    for i in range(2):
-        hit = (lane_of == expert) & (second == i)
-        spread_t[i] = jnp.where(hit, 1.0, 0.0).astype(BF16)
+    def spreads():
+        offset, second, _ = slots((LANES, ROWS), 1)
+        expert = owner(offset)
+        lane_of = lax.broadcasted_iota(jnp.int32, (LANES, ROWS), 0)
+        for i in range(2):
+            for j in range(2):
+                hit = (lane_of == expert + j * experts) & (second == i)
+                spread[2 * j + i] = jnp.where(hit, 1.0, 0.0).astype(BF16)
+        offset, second, _ = slots((ROWS, LANES), 0)
+        expert = owner(offset)
+        lane_of = lax.broadcasted_iota(jnp.int32, (ROWS, LANES), 1)
+        for i in range(2):
+            hit = (lane_of == expert) & (second == i)
+            spread_t[i] = jnp.where(hit, 1.0, 0.0).astype(BF16)
+
+    def early_pick():
+        q = lax.broadcasted_iota(jnp.int32, (PLANE * EARLY, LANES), 0)
+        lane_of = lax.broadcasted_iota(jnp.int32, (PLANE * EARLY, LANES), 1)
+        named = jnp.where(lane_of == owner(q >> 4), 1.0, 0.0).astype(BF16)
+        want = ((q & (EARLY - 1)) + 1).astype(F32)
+        return jnp.where(dot_nt(named, meta[0]) == want, 1.0, 0.0).astype(BF16)
 
     def few(step, direction):
         if step < FAR - 1:
@@ -200,7 +202,28 @@
 
     def dispatch(c, h):
         def send(offset, carry):
-            plane_copy(srow, rrow, d_send, d_recv, 1, offset, c, h).start()
+            if c:
+                plane_copy(srow, rrow, d_send, d_recv, 1, offset, c, h).start()
+                return carry
+            rows = pl.ds(pl.multiple_of(offset * PAIR + EARLY, 16), PAIR - EARLY)
+            pltpu.make_async_remote_copy(
+                srow.at[h, 0, rows], rrow.at[h, 0, rows], d_send.at[0, h], d_recv.at[0, h],
+                device_id={"expert": in_plane(1, offset)}, device_id_type=MESH,
+            ).start()
+            return carry
+
+        lax.fori_loop(1, PLANE, send, 0)
+
+    def dispatch_early(h, chosen):
+        erow[h] = dot(chosen, line[h, 0]).astype(BF16)
+
+        def send(offset, carry):
+            source = pl.ds(pl.multiple_of(offset * EARLY, 16), EARLY)
+            target = pl.ds(pl.multiple_of(offset * PAIR, 16), EARLY)
+            pltpu.make_async_remote_copy(
+                erow.at[h, source], rrow.at[h, 0, target], d_send.at[0, h], d_recv.at[0, h],
+                device_id={"expert": in_plane(1, offset)}, device_id_type=MESH,
+            ).start()
             return carry
 
         lax.fori_loop(1, PLANE, send, 0)
@@ -224,8 +247,7 @@
             for base in (0, hidden):
                 cols = pl.ds(pl.multiple_of(base + n * TILE, TILE), TILE)
                 total.append(
-                    dot(rrow[0, c], wup[pl.ds(0, part), cols])
-                    + dot(rrow[1, c], wup[pl.ds(part, part), cols])
+                    sum(dot(rrow[h, c], wup[pl.ds(h * part, part), cols]) for h in range(PARTS))
                 )
             g, u = total
             cols = pl.ds(pl.multiple_of(n * TILE, TILE), TILE)
@@ -290,13 +312,25 @@
             device_id={"section": following}, device_id_type=MESH,
         )
 
+    squares = jnp.zeros((tokens, BLOCK), F32)
+    for b in range(width // BLOCK):
+        values = x_ref[:, b * BLOCK : (b + 1) * BLOCK].astype(F32)
+        squares = squares + values * values
+    inverse = lax.rsqrt(jnp.sum(squares, axis=1, keepdims=True) / width + EPS)
+    restore(0)
+    route()
     pl.semaphore_wait(barrier, PLANE - 1 + 4)
-
-    for direction in range(2):
-        gather_meta(direction, 0).start()
-    for h in range(PARTS):
+    for h in range(PARTS):
+        if h:
+            restore(h)
         for direction in range(2):
             gather(direction, 0, h).start()
+            if h == 0:
+                gather_meta(direction, 0).start()
+        if h == 0:
+            chosen = early_pick()
+        dispatch_early(h, chosen)
+    spreads()
     for step in range(1, FAR + 1):
         c = step % FAR
         first, last = (step, NZ - step) if c else (0, FAR)
@@ -389,6 +423,7 @@
             pltpu.VMEM((PARTS, FAR, ROWS, part), BF16),
             pltpu.VMEM((PARTS, FAR, ROWS, part), BF16),
             pltpu.VMEM((PARTS, FAR, ROWS, part), BF16),
+            pltpu.VMEM((PARTS, PLANE * EARLY, part), BF16),
             pltpu.VMEM((FAR, 2 * tokens, ROWS), BF16),
             pltpu.VMEM((ROWS, 2 * tokens), BF16),
             pltpu.VMEM((4, LANES, ROWS), BF16),
@@ -419,7 +454,7 @@
             collective_id=0, has_side_effects=True, vmem_limit_bytes=62 << 20
         ),
         name="relay_step",
-    )(x, gain, final_gain[None], assigned[0], mixing[0], raising[0, 0], lowering[0, 0])
+    )(x, gain, final_gain[None], assigned[0].T, mixing[0].T, raising[0, 0], lowering[0, 0])
     return arrived[None]
 
 

time: 177 us -> 162 us (0.915); the launches traced: 174 us -> 161 us
  Pallas kernels: 169 us -> 159 us
  local copies, waits for them, and re-layouts: 4.7 us -> 1.88 us
    pallas_call x1, Pallas kernels: 169 us -> 159 us  [local(): pl.pallas_call(body, out_shape=jax.ShapeDtypeStruct((tokens, width), BF16...]
    unnamed x3 -> x1, local copies, waits for them, and re-layouts: 4.7 us -> 1.88 us
where the time goes in v3:
time: 162 us; the launch traced here: 161 us
  Pallas kernels  159 us (98%)
  local copies, waits for them, and re-layouts  1.88 us (1%)
    pallas_call x1, Pallas kernels, local(): pl.pallas_call(body, out_shape=jax.ShapeDtypeStruct((tokens, width), BF16...  159 us

profile of v3, /device:TPU:1, one launch (start us, length us, event | category | flops | bytes accessed | tf_op | source)
XLA Modules:
  0.0 160.7 jit_solution(16240900292335684556)
XLA Ops:
  0.0 158.8 %relay_step.1 = bf16[128,2048]{1,0:T(8,128)(2,1)} custom-call(bf16[128,2048]{1,0:T(8,128)(2,1)} %bitcast.14, f32[1,2048]{1,0:T(1,128)} %gain_ref.1, f32[1,2048]{1,0:T(1,128)} %bitcast.15, s32[8,128]{1,0:T(8,128)} %bitcast.16, f32[8,128]{1,0:T(8,128)} %bitcast.17, bf16[2048,1536]{1,0:T(8,128)(2,1)} %bitcast.11, bf16[768,2048]{1,0:T(8,128)(2,1)} %bitcast.12), custom_call_target="tpu_custom_call" | custom-call | tf_op jit(solution)/shard_map/relay_step/pallas_call | solution.py:414
  158.8 1.9 %copy.9 = bf16[1,128,2048]{2,1,0:T(8,128)(2,1)} copy(bf16[1,128,2048]{2,1,0:T(8,128)(2,1)} %bitcast.13) | data formatting | bytes 1048576

commit v4 on v3

--- a/solution.py
+++ b/solution.py
@@ -33,10 +33,10 @@
 
 def body(
     x_ref, gain_ref, final_ref, route_ref, mixing_ref, up_ref, down_ref, out_ref,
-    line, meta, srow, rrow, orow, ret, erow, mix, pick, spread, spread_t, wup, wdown, hid,
+    line, meta, srow, rrow, orow, ret, erow, lret, mix, mix_late, pick, spread, spread_t, wup, wdown, hid,
     acc, rsout, rsin, layer, arrive,
     ag_send, ag_recv, am_send, am_recv, d_send, d_recv, r_send, r_recv,
-    rs_send, rs_recv, sec_send, sec_recv, w_sem,
+    rs_send, rs_recv, sec_send, sec_recv, l_send, l_recv, w_sem,
 ):
     tokens, width = x_ref.shape
     part = width // PARTS
@@ -139,6 +139,21 @@
         want = ((q & (EARLY - 1)) + 1).astype(F32)
         return jnp.where(dot_nt(named, meta[0]) == want, 1.0, 0.0).astype(BF16)
 
+    def late_mix():
+        shape = (LANES, PLANE * EARLY)
+        q, lane_of = lax.broadcasted_iota(jnp.int32, shape, 1), lax.broadcasted_iota(jnp.int32, shape, 0)
+        expert = owner(q >> 4)
+        named = jnp.where(lane_of == expert, 1.0, 0.0).astype(BF16)
+        share = jnp.where(lane_of == expert + experts, 1.0, 0.0).astype(BF16)
+        q = lax.broadcasted_iota(jnp.int32, (tokens, PLANE * EARLY), 1)
+        want = ((q & (EARLY - 1)) + 1).astype(F32)
+        weight = dot(meta[0], share)
+        mix_late[...] = jnp.where(dot(meta[0], named) == want, weight, 0.0).astype(BF16)
+        for h in range(PARTS):
+            lret[h, pl.ds(0, EARLY)] = jnp.zeros((EARLY, part), BF16)
+            for offset in range(1, PLANE):
+                ret[h, 0, pl.ds(offset * PAIR, EARLY)] = jnp.zeros((EARLY, part), BF16)
+
     def few(step, direction):
         if step < FAR - 1:
             return pl.ds(0, tokens)
@@ -230,13 +245,50 @@
 
     def give_back(c, h):
         def send(offset, carry):
-            plane_copy(orow, ret, r_send, r_recv, -1, offset, c, h).start()
+            if c:
+                plane_copy(orow, ret, r_send, r_recv, -1, offset, c, h).start()
+                return carry
+            rows = pl.ds(pl.multiple_of(offset * PAIR + EARLY, 16), PAIR - EARLY)
+            pltpu.make_async_remote_copy(
+                orow.at[h, 0, rows], ret.at[h, 0, rows], r_send.at[0, h], r_recv.at[0, h],
+                device_id={"expert": in_plane(-1, offset)}, device_id_type=MESH,
+            ).start()
             return carry
 
         lax.fori_loop(1, PLANE, send, 0)
 
+    def late_copy(offset, h):
+        source = pl.ds(pl.multiple_of(offset * PAIR, 16), EARLY)
+        target = pl.ds(pl.multiple_of(offset * EARLY, 16), EARLY)
+        return pltpu.make_async_remote_copy(
+            orow.at[h, 0, source], lret.at[h, target], l_send.at[h], l_recv.at[h],
+            device_id={"expert": in_plane(-1, offset)}, device_id_type=MESH,
+        )
+
+    def give_back_late(h):
+        def send(offset, carry):
+            late_copy(offset, h).start()
+            return carry
+
+        lax.fori_loop(1, PLANE, send, 0)
+
+    def late(h):
+        rows, few = pl.ds(EARLY, (PLANE - 1) * EARLY), pl.ds(PAIR, (PLANE - 1) * EARLY)
+        return pltpu.make_async_remote_copy(
+            orow.at[h, 0, few], lret.at[h, rows], l_send.at[h], l_recv.at[h],
+            device_id={"expert": in_plane(-1, 1)}, device_id_type=MESH,
+        )
+
+    def returned(c, h):
+        if c:
+            return plane_all(orow, ret, r_send, r_recv, c, h)
+        rows = pl.ds(PAIR, (PLANE - 1) * (PAIR - EARLY))
+        return pltpu.make_async_remote_copy(
+            orow.at[h, 0, rows], ret.at[h, 0, rows], r_send.at[0, h], r_recv.at[0, h],
+            device_id={"expert": in_plane(-1, 1)}, device_id_type=MESH,
+        )
+
     dispatched = functools.partial(plane_all, srow, rrow, d_send, d_recv)
-    given_back = functools.partial(plane_all, orow, ret, r_send, r_recv)
 
     def expert_rows(c):
         for h in range(PARTS):
@@ -277,7 +329,7 @@
 
     def combine(c, h):
         step = FAR - c if c else 0
-        given_back(c, h).wait_recv()
+        returned(c, h).wait_recv()
         if step:
             for direction in range(2):
                 scatter(direction, step - 1, h).wait_recv()
@@ -331,6 +383,7 @@
             chosen = early_pick()
         dispatch_early(h, chosen)
     spreads()
+    late_mix()
     for step in range(1, FAR + 1):
         c = step % FAR
         first, last = (step, NZ - step) if c else (0, FAR)
@@ -359,6 +412,8 @@
     for c in range(FAR - 2, 0, -1):
         for h in range(PARTS):
             give_back(c, h)
+    for h in range(PARTS):
+        give_back_late(h)
     for c in (0, *range(FAR - 1, 0, -1)):
         for h in range(PARTS):
             combine(c, h)
@@ -366,6 +421,8 @@
         for direction in range(2):
             scatter(direction, FAR - 1, h).wait_recv()
         total = acc[h] + rsin[h, 0, FAR - 1].astype(F32) + rsin[h, 1, FAR - 1].astype(F32)
+        late(h).wait_recv()
+        total = total + dot(mix_late[...], lret[h])
         layer[h] = total.astype(BF16)
         onward(h).start()
     for h in range(PARTS):
@@ -396,8 +453,9 @@
                 scatter(direction, step, h).wait_send()
         for c in range(FAR):
             dispatched(c, h).wait_send()
-            given_back(c, h).wait_send()
+            returned(c, h).wait_send()
         onward(h).wait_send()
+        late(h).wait_send()
     for step in range(FAR):
         for direction in range(2):
             gather_meta(direction, step).wait_send()
@@ -424,7 +482,9 @@
             pltpu.VMEM((PARTS, FAR, ROWS, part), BF16),
             pltpu.VMEM((PARTS, FAR, ROWS, part), BF16),
             pltpu.VMEM((PARTS, PLANE * EARLY, part), BF16),
+            pltpu.VMEM((PARTS, PLANE * EARLY, part), BF16),
             pltpu.VMEM((FAR, 2 * tokens, ROWS), BF16),
+            pltpu.VMEM((tokens, PLANE * EARLY), BF16),
             pltpu.VMEM((ROWS, 2 * tokens), BF16),
             pltpu.VMEM((4, LANES, ROWS), BF16),
             pltpu.VMEM((2, ROWS, LANES), BF16),
@@ -448,6 +508,8 @@
             sems((2, FAR, PARTS)),
             sems((PARTS,)),
             sems((PARTS,)),
+            sems((PARTS,)),
+            sems((PARTS,)),
             sems((2,)),
         ],
         compiler_params=pltpu.CompilerParams(

time: 162 us -> 159 us (0.981)
  Pallas kernels: 159 us -> 156 us
    pallas_call x1, Pallas kernels: 159 us -> 156 us  [local(): pl.pallas_call(body, out_shape=jax.ShapeDtypeStruct((tokens, width), BF16...]
where the time goes in v4:
time: 159 us; the launch traced here: 158 us
  Pallas kernels  156 us (98%)
  local copies, waits for them, and re-layouts  1.88 us (1%)
    pallas_call x1, Pallas kernels, local(): pl.pallas_call(body, out_shape=jax.ShapeDtypeStruct((tokens, width), BF16...  156 us

profile of v4, /device:TPU:1, one launch (start us, length us, event | category | flops | bytes accessed | tf_op | source)
XLA Modules:
  0.0 158.0 jit_solution(6216772310122861804)
XLA Ops:
  0.0 156.1 %relay_step.1 = bf16[128,2048]{1,0:T(8,128)(2,1)} custom-call(bf16[128,2048]{1,0:T(8,128)(2,1)} %bitcast.14, f32[1,2048]{1,0:T(1,128)} %gain_ref.1, f32[1,2048]{1,0:T(1,128)} %bitcast.15, s32[8,128]{1,0:T(8,128)} %bitcast.16, f32[8,128]{1,0:T(8,128)} %bitcast.17, bf16[2048,1536]{1,0:T(8,128)(2,1)} %bitcast.11, bf16[768,2048]{1,0:T(8,128)(2,1)} %bitcast.12), custom_call_target="tpu_custom_call" | custom-call | tf_op jit(solution)/shard_map/relay_step/pallas_call | solution.py:472
  156.1 1.9 %copy.9 = bf16[1,128,2048]{2,1,0:T(8,128)(2,1)} copy(bf16[1,128,2048]{2,1,0:T(8,128)(2,1)} %bitcast.13) | data formatting | bytes 1048576

commit v5 on v4

--- a/solution.py
+++ b/solution.py
@@ -32,11 +32,11 @@
 
 
 def body(
-    x_ref, gain_ref, final_ref, route_ref, mixing_ref, up_ref, down_ref, out_ref,
-    line, meta, srow, rrow, orow, ret, erow, lret, mix, mix_late, pick, spread, spread_t, wup, wdown, hid,
-    acc, rsout, rsin, layer, arrive,
+    x_hbm, gain_ref, final_ref, route_ref, mixing_ref, up_ref, down_ref, out_ref,
+    x_ref, line, meta, srow, rrow, orow, ret, erow, lret, mix, mix_late, pick, spread, spread_t, wup, wdown, hid,
+    acc, rsout, rsin, layer, arrive, normed,
     ag_send, ag_recv, am_send, am_recv, d_send, d_recv, r_send, r_recv,
-    rs_send, rs_recv, sec_send, sec_recv, l_send, l_recv, w_sem,
+    rs_send, rs_recv, sec_send, sec_recv, l_send, l_recv, o_sem, w_sem,
 ):
     tokens, width = x_ref.shape
     part = width // PARTS
@@ -60,12 +60,12 @@
     following = (section + 1) % sections
     previous = (section + sections - 1) % sections
 
+    load = pltpu.make_async_copy(x_hbm, x_ref, w_sem.at[2])
+    load.start()
     weights = [
         pltpu.make_async_copy(up_ref, wup, w_sem.at[0]),
         pltpu.make_async_copy(down_ref, wdown, w_sem.at[1]),
     ]
-    for copy in weights:
-        copy.start()
 
     barrier = pltpu.get_barrier_semaphore()
 
@@ -358,19 +358,29 @@
         for direction in range(2):
             scatter(direction, step, h).start()
 
-    def onward(h):
-        return pltpu.make_async_remote_copy(
-            layer.at[h], arrive.at[h], sec_send.at[h], sec_recv.at[h],
+    pieces = [(h, slice(0, part)) for h in range(PARTS - 1)]
+    pieces += [(PARTS - 1, slice(0, part // 2)), (PARTS - 1, slice(part // 2, part))]
+
+    def onward(i):
+        h, cols = pieces[i]
+        return pltpu.make_async_remote_copy(
+            layer.at[h, :, cols], arrive.at[h, :, cols], sec_send.at[i], sec_recv.at[i],
             device_id={"section": following}, device_id_type=MESH,
         )
 
+    def put(source, i):
+        h, cols = pieces[i]
+        place = slice(h * part + cols.start, h * part + cols.stop)
+        return pltpu.make_async_copy(source.at[h, :, cols], out_ref.at[:, place], o_sem.at[i])
+
+    route()
+    load.wait()
     squares = jnp.zeros((tokens, BLOCK), F32)
     for b in range(width // BLOCK):
         values = x_ref[:, b * BLOCK : (b + 1) * BLOCK].astype(F32)
         squares = squares + values * values
     inverse = lax.rsqrt(jnp.sum(squares, axis=1, keepdims=True) / width + EPS)
     restore(0)
-    route()
     pl.semaphore_wait(barrier, PLANE - 1 + 4)
     for h in range(PARTS):
         if h:
@@ -382,6 +392,8 @@
         if h == 0:
             chosen = early_pick()
         dispatch_early(h, chosen)
+    for copy in weights:
+        copy.start()
     spreads()
     late_mix()
     for step in range(1, FAR + 1):
@@ -417,34 +429,42 @@
     for c in (0, *range(FAR - 1, 0, -1)):
         for h in range(PARTS):
             combine(c, h)
-    for h in range(PARTS):
-        for direction in range(2):
-            scatter(direction, FAR - 1, h).wait_recv()
-        total = acc[h] + rsin[h, 0, FAR - 1].astype(F32) + rsin[h, 1, FAR - 1].astype(F32)
-        late(h).wait_recv()
-        total = total + dot(mix_late[...], lret[h])
-        layer[h] = total.astype(BF16)
-        onward(h).start()
-    for h in range(PARTS):
-        onward(h).wait_recv()
+    for i, (h, cols) in enumerate(pieces):
+        if cols.start == 0:
+            for direction in range(2):
+                scatter(direction, FAR - 1, h).wait_recv()
+            late(h).wait_recv()
+        total = acc[h, :, cols] + rsin[h, 0, FAR - 1, :, cols].astype(F32)
+        total = total + rsin[h, 1, FAR - 1, :, cols].astype(F32)
+        total = total + dot(mix_late[...], lret[h, :, cols])
+        layer[h, :, cols] = total.astype(BF16)
+        onward(i).start()
 
     @pl.when(section != 0)
     def _():
-        for h in range(PARTS):
-            out_ref[:, h * part : (h + 1) * part] = arrive[h]
+        for i in range(len(pieces)):
+            onward(i).wait_recv()
+            put(arrive, i).start()
+        for i in range(len(pieces)):
+            put(arrive, i).wait()
 
     @pl.when(section == 0)
     def _():
         squares = jnp.zeros((tokens, BLOCK), F32)
-        for b in range(width // BLOCK):
-            place = (b % per_part) * BLOCK
-            values = arrive[b // per_part, :, place : place + BLOCK].astype(F32)
-            squares = squares + values * values
+        for i, (h, cols) in enumerate(pieces):
+            onward(i).wait_recv()
+            for place in range(cols.start, cols.stop, BLOCK):
+                values = arrive[h, :, place : place + BLOCK].astype(F32)
+                squares = squares + values * values
         inverse = lax.rsqrt(jnp.sum(squares, axis=1, keepdims=True) / width + EPS)
-        for b in range(width // BLOCK):
-            place, cols = (b % per_part) * BLOCK, slice(b * BLOCK, (b + 1) * BLOCK)
-            values = arrive[b // per_part, :, place : place + BLOCK].astype(F32)
-            out_ref[:, cols] = (values * inverse * final_ref[:, cols]).astype(BF16)
+        for i, (h, cols) in enumerate(pieces):
+            for place in range(cols.start, cols.stop, BLOCK):
+                values = arrive[h, :, place : place + BLOCK].astype(F32)
+                gain = final_ref[:, h * part + place : h * part + place + BLOCK]
+                normed[h, :, place : place + BLOCK] = (values * inverse * gain).astype(BF16)
+            put(normed, i).start()
+        for i in range(len(pieces)):
+            put(normed, i).wait()
 
     for h in range(PARTS):
         for step in range(FAR):
@@ -454,8 +474,9 @@
         for c in range(FAR):
             dispatched(c, h).wait_send()
             returned(c, h).wait_send()
-        onward(h).wait_send()
         late(h).wait_send()
+    for i in range(len(pieces)):
+        onward(i).wait_send()
     for step in range(FAR):
         for direction in range(2):
             gather_meta(direction, step).wait_send()
@@ -472,9 +493,10 @@
     arrived = pl.pallas_call(
         body,
         out_shape=jax.ShapeDtypeStruct((tokens, width), BF16),
-        in_specs=[vmem, vmem, vmem, vmem, vmem, hbm, hbm],
-        out_specs=vmem,
+        in_specs=[hbm, vmem, vmem, vmem, vmem, hbm, hbm],
+        out_specs=hbm,
         scratch_shapes=[
+            pltpu.VMEM((tokens, width), BF16),
             pltpu.VMEM((PARTS, NZ, tokens, part), BF16),
             pltpu.VMEM((NZ, tokens, LANES), BF16),
             pltpu.VMEM((PARTS, FAR, ROWS, part), BF16),
@@ -496,6 +518,7 @@
             pltpu.VMEM((PARTS, 2, FAR, tokens, part), BF16),
             pltpu.VMEM((PARTS, tokens, part), BF16),
             pltpu.VMEM((PARTS, tokens, part), BF16),
+            pltpu.VMEM((PARTS, tokens, part), BF16),
             sems((2, FAR, PARTS)),
             sems((2, FAR, PARTS)),
             sems((2, FAR)),
@@ -506,11 +529,12 @@
             sems((FAR, PARTS)),
             sems((2, FAR, PARTS)),
             sems((2, FAR, PARTS)),
+            sems((PARTS + 1,)),
+            sems((PARTS + 1,)),
             sems((PARTS,)),
             sems((PARTS,)),
-            sems((PARTS,)),
-            sems((PARTS,)),
-            sems((2,)),
+            sems((PARTS + 1,)),
+            sems((3,)),
         ],
         compiler_params=pltpu.CompilerParams(
             collective_id=0, has_side_effects=True, vmem_limit_bytes=62 << 20

time: 159 us -> 158 us (level)
  no operation moved by 1% of the time
where the time goes in v5:
time: 158 us; the launch traced here: 157 us
  Pallas kernels  155 us (98%)
  local copies, waits for them, and re-layouts  1.88 us (1%)
    pallas_call x1, Pallas kernels, local(): pl.pallas_call(body, out_shape=jax.ShapeDtypeStruct((tokens, width), BF16...  155 us

profile of v5, /device:TPU:1, one launch (start us, length us, event | category | flops | bytes accessed | tf_op | source)
XLA Modules:
  0.0 156.9 jit_solution(10352253674937615245)
XLA Ops:
  0.0 155.0 %relay_step.1 = bf16[128,2048]{1,0:T(8,128)(2,1)} custom-call(bf16[128,2048]{1,0:T(8,128)(2,1)} %bitcast.14, f32[1,2048]{1,0:T(1,128)} %gain_ref.1, f32[1,2048]{1,0:T(1,128)} %bitcast.15, s32[8,128]{1,0:T(8,128)} %bitcast.16, f32[8,128]{1,0:T(8,128)} %bitcast.17, bf16[2048,1536]{1,0:T(8,128)(2,1)} %bitcast.11, bf16[768,2048]{1,0:T(8,128)(2,1)} %bitcast.12), custom_call_target="tpu_custom_call" | custom-call | tf_op jit(solution)/shard_map/relay_step/pallas_call | solution.py:493
  155.0 1.9 %copy.9 = bf16[1,128,2048]{2,1,0:T(8,128)(2,1)} copy(bf16[1,128,2048]{2,1,0:T(8,128)(2,1)} %bitcast.13) | data formatting | bytes 1048576

commit v6 on v5

--- a/solution.py
+++ b/solution.py
@@ -308,15 +308,19 @@
 
         lax.fori_loop(0, hidden // TILE, gate, 0)
 
-        def lower(n, carry):
-            wide = pl.ds(pl.multiple_of(n * TILE, TILE), TILE)
-            cols = pl.ds(pl.multiple_of((n % tiles) * TILE, TILE), TILE)
-            rows = dot(hid[...], wdown[:, wide]).astype(BF16)
-            orow[n // tiles, c, :, cols] = rows
-            ret[n // tiles, c, pl.ds(0, PAIR), cols] = rows[:PAIR]
-            return carry
-
-        lax.fori_loop(0, PARTS * tiles, lower, 0)
+        for h in range(PARTS):
+
+            def lower(n, carry):
+                cols = pl.ds(pl.multiple_of(n * TILE, TILE), TILE)
+                wide = pl.ds(pl.multiple_of(h * part + n * TILE, TILE), TILE)
+                rows = dot(hid[...], wdown[:, wide]).astype(BF16)
+                orow[h, c, :, cols] = rows
+                ret[h, c, pl.ds(0, PAIR), cols] = rows[:PAIR]
+                return carry
+
+            lax.fori_loop(0, tiles, lower, 0)
+            if c in (0, FAR - 1):
+                give_back(c, h)
 
     def scatter(direction, step, h):
         source = FAR - step if direction == 0 else FAR + step
@@ -416,11 +420,7 @@
         copy.wait()
     for c in range(1, FAR):
         expert_rows(c)
-    for h in range(PARTS):
-        give_back(FAR - 1, h)
     expert_rows(0)
-    for h in range(PARTS):
-        give_back(0, h)
     for c in range(FAR - 2, 0, -1):
         for h in range(PARTS):
             give_back(c, h)

time: 158 us -> 158 us (level)
  no operation moved by 1% of the time
where the time goes in v6:
time: 158 us; the launch traced here: 157 us
  Pallas kernels  155 us (98%)
  local copies, waits for them, and re-layouts  1.88 us (1%)
    pallas_call x1, Pallas kernels, local(): pl.pallas_call(body, out_shape=jax.ShapeDtypeStruct((tokens, width), BF16...  155 us

profile of v6, /device:TPU:1, one launch (start us, length us, event | category | flops | bytes accessed | tf_op | source)
XLA Modules:
  0.0 156.8 jit_solution(11161171669297491922)
XLA Ops:
  0.0 154.9 %relay_step.1 = bf16[128,2048]{1,0:T(8,128)(2,1)} custom-call(bf16[128,2048]{1,0:T(8,128)(2,1)} %bitcast.14, f32[1,2048]{1,0:T(1,128)} %gain_ref.1, f32[1,2048]{1,0:T(1,128)} %bitcast.15, s32[8,128]{1,0:T(8,128)} %bitcast.16, f32[8,128]{1,0:T(8,128)} %bitcast.17, bf16[2048,1536]{1,0:T(8,128)(2,1)} %bitcast.11, bf16[768,2048]{1,0:T(8,128)(2,1)} %bitcast.12), custom_call_target="tpu_custom_call" | custom-call | tf_op jit(solution)/shard_map/relay_step/pallas_call | solution.py:493
  154.9 1.9 %copy.9 = bf16[1,128,2048]{2,1,0:T(8,128)(2,1)} copy(bf16[1,128,2048]{2,1,0:T(8,128)(2,1)} %bitcast.13) | data formatting | bytes 1048576
